TPU v7x, 128 devices: a whole 4x4x4 slice. The times are simulated.
128 devices in a mesh: expert: 8 (over z_lo, y), dp: 16 (over z_hi, x, core).
Axes of the slice: x: 4, y: 4, z: 4 (z_hi: 2, z_lo: 2; z = z_hi * 2 + z_lo), core: 2. Of those that a mesh axis runs over, the one named last changes fastest.
Arguments:
- tokens: bfloat16 [2048, 7168], P('dp', 'expert'), may hold values from -6 to 6
- grad_out: bfloat16 [2048, 7168], P('dp', 'expert'), may hold values from -6 to 6
- expert_ids: int32 [2048, 2], P('dp'), may hold values from -1 to 7, as said below
- route_weights: float32 [2048, 2], P('dp'), may hold values from 0.1 to 1
- w_gate: bfloat16 [8, 7168, 2048], P('expert', 'dp'), may hold values from -0.0625 to 0.0625
- w_up: bfloat16 [8, 7168, 2048], P('expert', 'dp'), may hold values from -0.0625 to 0.0625
- w_down: bfloat16 [8, 2048, 7168], P('expert', None, 'dp'), may hold values from -0.125 to 0.125
Outputs:
- grad_tokens: bfloat16 [2048, 7168], P('dp', 'expert')
- grad_gate: bfloat16 [8, 7168, 2048], P('expert', 'dp')
- grad_up: bfloat16 [8, 7168, 2048], P('expert', 'dp')
- grad_down: bfloat16 [8, 2048, 7168], P('expert', None, 'dp')
Inputs may be any that keep to these rules, and one draw needn't show every extreme that they name: expert_ids[t, 0] is an expert; expert_ids[t, 1] is another expert or -1. Within each block of 128 rows (the tokens of one index of dp) no expert appears in more than 64 rows, and one expert, the same in every block, appears in exactly 64 rows, each of which has -1 as its second entry.
All inputs are finite; a program needn't handle non-finite values.
Results may differ from a plain program's by a relative error of at most 0.03.
Values may be sent and summed in bfloat16 or wider, within the bound.
A program may use at most 128 MiB of HBM per device.

v0:
```python
import math
import jax
import jax.numpy as jnp
from jax import lax
from jax.sharding import PartitionSpec as P


def body(tokens, grad_out, expert_ids, route_weights, w_gate, w_up, w_down):
    experts = lax.axis_size("expert")
    groups = lax.axis_size("dp")
    tok_rows = tokens.shape[0]
    capacity = tok_rows // 2
    hidden = w_gate.shape[2]
    slots = groups * capacity
    expert_index = lax.axis_index("expert")
    inv_root = 1.0 / math.sqrt(tok_rows * groups)
    rows_first = (((0,), (0,)), ((), ()))
    last_dims = (((1,), (1,)), ((), ()))
    routed = expert_ids >= 0
    matches = (
        expert_ids[:, :, None] == jnp.arange(experts, dtype=jnp.int32)[None, None, :]
    ).astype(jnp.int32)
    flat_match = matches.reshape(tok_rows * 2, experts)
    position = jnp.sum(flat_match * (jnp.cumsum(flat_match, axis=0) - 1), axis=1).reshape(
        tok_rows, 2
    )
    slot_ids = jnp.where(routed, expert_ids * capacity + position, -1)
    slot_match = (
        slot_ids[None, :, :] == jnp.arange(experts * capacity, dtype=jnp.int32)[:, None, None]
    ).astype(jnp.float32)
    dispatch = jnp.sum(slot_match, axis=2).astype(jnp.bfloat16)
    slot_weight = jnp.einsum("stk,tk->s", slot_match, route_weights)
    own_weight = lax.dynamic_slice_in_dim(slot_weight, expert_index * capacity, capacity)
    send_x = (
        jnp.dot(dispatch, tokens, preferred_element_type=jnp.float32)
        .astype(jnp.bfloat16)
        .reshape(experts, capacity, -1)
    )
    send_g = (
        jnp.dot(dispatch, grad_out, preferred_element_type=jnp.float32)
        .astype(jnp.bfloat16)
        .reshape(experts, capacity, -1)
    )
    recv_x, recv_g = (
        lax.all_to_all(
            lax.all_to_all(send_x, "expert", split_axis=0, concat_axis=2, tiled=True),
            "dp",
            split_axis=2,
            concat_axis=1,
            tiled=True,
        ),
        lax.all_to_all(
            lax.all_to_all(send_g, "expert", split_axis=0, concat_axis=2, tiled=True),
            "dp",
            split_axis=2,
            concat_axis=1,
            tiled=True,
        ),
    )
    feature_rows = recv_x.reshape(slots, -1)
    grad_rows = recv_g.reshape(slots, -1)
    gate_shard = w_gate[0]
    up_shard = w_up[0]
    down_shard = w_down[0]
    shard_width = gate_shard.shape[0]
    x_block = feature_rows
    g_block = grad_rows
    gate = jnp.dot(x_block, gate_shard, preferred_element_type=jnp.float32)
    upper = jnp.dot(x_block, up_shard, preferred_element_type=jnp.float32)
    back = lax.dot_general(g_block, down_shard, last_dims, preferred_element_type=jnp.float32)
    mine = lax.psum_scatter(
        jnp.concatenate([gate, upper, back], axis=1).astype(jnp.bfloat16),
        "dp",
        scatter_dimension=0,
        tiled=True,
    ).astype(jnp.float32)
    gate = mine[:, :hidden]
    upper = mine[:, hidden : 2 * hidden]
    back = mine[:, 2 * hidden :] * own_weight[:, None]
    sigmoid_gate = jax.nn.sigmoid(gate)
    scaled = own_weight[:, None] * gate * sigmoid_gate * upper
    d_gate = back * upper * sigmoid_gate * (1.0 + gate * (1.0 - sigmoid_gate))
    d_up = back * gate * sigmoid_gate
    local = jnp.concatenate([scaled, d_gate, d_up], axis=1).astype(jnp.bfloat16)
    piece = lax.all_gather(local, "dp", axis=0, tiled=True)
    x_block = feature_rows
    g_block = grad_rows
    scaled = piece[:, :hidden]
    d_gate = piece[:, hidden : 2 * hidden]
    d_up = piece[:, 2 * hidden :]
    grad_g = lax.dot_general(x_block, d_gate, rows_first, preferred_element_type=jnp.float32)
    grad_u = lax.dot_general(x_block, d_up, rows_first, preferred_element_type=jnp.float32)
    grad_d = lax.dot_general(scaled, g_block, rows_first, preferred_element_type=jnp.float32)
    block_dx = lax.dot_general(
        d_gate, gate_shard, last_dims, preferred_element_type=jnp.float32
    ) + lax.dot_general(d_up, up_shard, last_dims, preferred_element_type=jnp.float32)
    dx_rows = block_dx.astype(jnp.bfloat16)
    grad_g, grad_u, grad_d, dx_rows = (grad_g, grad_u, grad_d, dx_rows)
    returned = lax.all_to_all(
        lax.all_to_all(
            dx_rows.reshape(1, slots, shard_width), "dp", split_axis=1, concat_axis=2, tiled=True
        ),
        "expert",
        split_axis=2,
        concat_axis=0,
        tiled=True,
    )
    returned = returned.reshape(experts * capacity, -1)
    grad_tokens = lax.dot_general(
        dispatch, returned, rows_first, preferred_element_type=jnp.float32
    ).astype(jnp.bfloat16)
    grad_gate = (grad_g * inv_root).astype(jnp.bfloat16)[None]
    grad_up = (grad_u * inv_root).astype(jnp.bfloat16)[None]
    grad_down = (grad_d * inv_root).astype(jnp.bfloat16)[None]
    return (grad_tokens, grad_gate, grad_up, grad_down)


def solution(mesh):
    in_specs = (
        P("dp", "expert"),
        P("dp", "expert"),
        P("dp", None),
        P("dp", None),
        P("expert", "dp", None),
        P("expert", "dp", None),
        P("expert", None, "dp"),
    )
    out_specs = (
        P("dp", "expert"),
        P("expert", "dp", None),
        P("expert", "dp", None),
        P("expert", None, "dp"),
    )
    return jax.shard_map(body, mesh=mesh, in_specs=in_specs, out_specs=out_specs, check_vma=False)
```

profile of v0, /device:TPU:1, one launch (start us, length us, event | category | flops | bytes accessed | tf_op | source)
XLA Modules:
  0.0 595.4 jit_solution(15682744833489243268)
XLA Ops:
  7.2 0.9 copy.79
  8.4 0.6 reduce-window.6
  9.0 0.2 slice_reduce_fusion
  9.6 0.7 compare_select_fusion
  10.3 2.3 convolution_convert_fusion.3
  12.6 6.4 %all-to-all-start.2 = ((bf16[8,64,896]{2,1,0:T(8,128)(2,1)}), bf16[8,64,896]{2,1,0:T(8,128)(2,1)S(1)}, u32[]{:S(2)}, u32[]{:S(2)}) async-start(bf16[8,64,896]{2,1,0:T(8,128)(2,1)} %bitcast.12), calls=%async_computation.2 | async-start | bytes 1835008 | tf_op jit(solution)/shard_map/all_to_all | solution.py:53
  19.0 1.3 convolution_convert_fusion.4
  20.3 13.1 %all-to-all-done.2 = bf16[8,64,896]{2,1,0:T(8,128)(2,1)S(1)} async-done(((bf16[8,64,896]{2,1,0:T(8,128)(2,1)}), bf16[8,64,896]{2,1,0:T(8,128)(2,1)S(1)}, u32[]{:S(2)}, u32[]{:S(2)}) %all-to-all-start.2) | async-done | bytes 917536 | tf_op jit(solution)/shard_map/all_to_all | solution.py:53
  33.4 0.9 copy-done.1
  34.3 3.6 all-to-all-start
  37.9 2.6 copy.97
  40.4 11.1 %reshape.65 = bf16[1,64,7168]{1,0,2:T(2,128)(2,1)} reshape(bf16[1,64,8,896]{1,3,2,0:T(8,128)(2,1)} %copy.97) | data formatting | bytes 1835008 | tf_op jit(solution)/shard_map/all_to_all | solution.py:53
  51.6 0.5 broadcast.46
  52.1 41.0 %reduce.2 = bf16[7168,64]{1,0:T(8,128)(2,1)} reduce(bf16[7168,1,64]{2,1,0:T(2,128)(2,1)} %bitcast.92, bf16[]{:T(256)} %broadcast.46), dimensions={1}, to_apply=%bitcast.70.reduce_sub_computation | reduce | bytes 1835010
  93.1 4.3 reshape.68
  97.3 8.5 %all-to-all-start.3 = ((bf16[16,2,14336]{2,1,0:T(2,128)(2,1)}), bf16[16,2,14336]{2,1,0:T(2,128)(2,1)}, u32[]{:S(2)}, u32[]{:S(2)}) async-start(bf16[16,2,14336]{2,1,0:T(2,128)(2,1)} %reshape.68), calls=%async_computation.3 | async-start | bytes 1835008 | tf_op jit(solution)/shard_map/all_to_all | solution.py:52
  105.9 1.7 copy.96
  107.5 11.1 %reshape.64 = bf16[1,64,7168]{1,0,2:T(2,128)(2,1)} reshape(bf16[1,64,8,896]{1,3,2,0:T(8,128)(2,1)} %copy.96) | data formatting | bytes 1835008 | tf_op jit(solution)/shard_map/all_to_all | solution.py:46
  118.7 41.0 %reduce.3 = bf16[7168,64]{1,0:T(8,128)(2,1)} reduce(bf16[7168,1,64]{2,1,0:T(2,128)(2,1)} %bitcast.94, bf16[]{:T(256)} %broadcast.46), dimensions={1}, to_apply=%bitcast.72.reduce_sub_computation | reduce | bytes 1835010
  159.7 4.3 reshape.70
  163.9 7.2 %all-to-all-start.1 = ((bf16[16,2,14336]{2,1,0:T(2,128)(2,1)}), bf16[16,2,14336]{2,1,0:T(2,128)(2,1)}, u32[]{:S(2)}, u32[]{:S(2)}) async-start(bf16[16,2,14336]{2,1,0:T(2,128)(2,1)} %reshape.70), calls=%async_computation.1 | async-start | bytes 1835008 | tf_op jit(solution)/shard_map/all_to_all | solution.py:45
  171.2 0.4 reduce-scatter.2.cloned.1.call-start
  171.6 9.9 %reshape.69 = bf16[7168,1,64]{2,1,0:T(2,128)(2,1)} reshape(bf16[16,2,14336]{2,1,0:T(2,128)(2,1)} %all-to-all-done.3) | data formatting | bytes 1835008
  181.5 8.1 %copy.88 = bf16[1,64,7168]{2,1,0:T(8,128)(2,1)} copy(bf16[1,64,7168]{1,0,2:T(2,128)(2,1)} %bitcast.95) | data formatting | bytes 1835008 | tf_op jit(solution)/shard_map/all_to_all | solution.py:52
  189.7 2.3 all_to_all.84
  192.0 1.6 copy.89
  193.6 9.9 %reshape.71 = bf16[7168,1,64]{2,1,0:T(2,128)(2,1)} reshape(bf16[16,2,14336]{2,1,0:T(2,128)(2,1)} %all-to-all-done.1) | data formatting | bytes 1835008
  203.5 8.1 %copy.84 = bf16[1,64,7168]{2,1,0:T(8,128)(2,1)} copy(bf16[1,64,7168]{1,0,2:T(2,128)(2,1)} %bitcast.96) | data formatting | bytes 1835008 | tf_op jit(solution)/shard_map/all_to_all | solution.py:45
  211.7 2.3 all_to_all.77
  214.0 0.6 copy.85
  214.6 2.3 convolution_convert_fusion.1
  217.0 2.3 convolution_convert_fusion.2
  219.4 2.3 convolution_convert_fusion
  221.7 11.3 %pad_maximum_fusion = bf16[1024,6144]{1,0:T(8,128)(2,1)} fusion(bf16[1024,2048]{1,0:T(8,128)(2,1)S(1)} %convolution_convert_fusion, bf16[1024,2048]{1,0:T(8,128)(2,1)S(1)} %convolution_convert_fusion.1, bf16[1024,2048]{1,0:T(8,128)(2,1)S(1)} %convolution_convert_fusion.2), kind=kLoop, calls=%fused_computation | loop fusion | flops 37748736 | bytes 25165824 | tf_op jit(solution)/shard_map/concatenate | solution.py:72
  233.0 0.2 all-gather.2.cloned.1.call-start
  233.3 0.4 copy-done.9
  233.7 0.2 fusion.39
  234.0 122.2 %reduce-scatter.2.cloned.1.call-done = bf16[64,6144]{1,0:T(8,128)(2,1)} async-done(((bf16[1024,6144]{1,0:T(8,128)(2,1)}), bf16[64,6144]{1,0:T(8,128)(2,1)}) %reduce-scatter.2.cloned.1.call-update) | async-done | bytes 786448 | tf_op jit(solution)/shard_map/reduce_scatter | solution.py:71
  356.2 1.2 convert_element_type.43
  357.4 0.4 multiply_convert_fusion.5
  357.8 0.9 pad_maximum_fusion.1
  358.8 91.2 %all-gather.2.cloned.1.call-done = bf16[1024,6144]{1,0:T(8,128)(2,1)} async-done(((bf16[64,6144]{1,0:T(8,128)(2,1)}), bf16[1024,6144]{1,0:T(8,128)(2,1)}) %all-gather.2.cloned.1.call-update) | async-done | bytes 12582928 | tf_op jit(solution)/shard_map/all_gather | solution.py:85
  449.9 4.4 fusion.4
  454.3 4.4 fusion.34
  458.7 3.9 copy.90
  462.6 8.3 %reduce.4 = bf16[1024,448]{1,0:T(8,128)(2,1)S(1)} reduce(bf16[1024,1,448]{2,1,0:T(2,128)(2,1)} %bitcast.98, bf16[]{:T(256)} %broadcast.46), dimensions={1}, to_apply=%bitcast.74.reduce_sub_computation | reduce | bytes 1835010
  470.9 2.1 reshape.72
  473.0 3.9 all-to-all-start.4
  476.9 5.8 fusion.16
  482.7 10.2 %all-to-all-done.4 = bf16[16,2,14336]{2,1,0:T(2,128)(2,1)S(1)} async-done(((bf16[16,2,14336]{2,1,0:T(2,128)(2,1)}), bf16[16,2,14336]{2,1,0:T(2,128)(2,1)S(1)}, u32[]{:S(2)}, u32[]{:S(2)}) %all-to-all-start.4) | async-done | bytes 917536 | tf_op jit(solution)/shard_map/all_to_all | solution.py:100
  492.9 3.7 reshape.73
  496.6 1.9 copy.102
  498.5 1.7 copy.98
  500.2 11.1 %reshape.66 = bf16[1,64,7168]{1,0,2:T(2,128)(2,1)} reshape(bf16[1,64,16,448]{1,3,2,0:T(8,128)(2,1)} %copy.98) | data formatting | bytes 1835008 | tf_op jit(solution)/shard_map/all_to_all | solution.py:100
  511.3 41.0 %reduce.5 = bf16[7168,64]{1,0:T(8,128)(2,1)} reduce(bf16[7168,1,64]{2,1,0:T(2,128)(2,1)} %bitcast.93, bf16[]{:T(256)} %broadcast.46), dimensions={1}, to_apply=%bitcast.76.reduce_sub_computation | reduce | bytes 1835010
  552.3 4.3 reshape.74
  556.6 4.4 all-to-all-start.5
  561.0 5.9 fusion.19
  566.9 5.5 fusion.22
  572.5 2.9 all-to-all-done.5
  575.4 4.1 reshape.75
  579.5 7.2 %copy.93 = bf16[1,64,7168]{2,1,0:T(8,128)(2,1)S(1)} copy(bf16[1,64,7168]{1,0,2:T(2,128)(2,1)} %bitcast.97) | data formatting | bytes 1835008 | tf_op jit(solution)/shard_map/all_to_all | solution.py:99
  586.7 0.1 copy.103
  587.1 1.0 convolution_convert_fusion.5
  (35 shorter events, 1.1 us)
Async XLA Ops:
  7.2 207.4 %copy-start = (bf16[1,448,2048]{2,1,0:T(8,128)(2,1)S(1)}, bf16[1,448,2048]{2,1,0:T(8,128)(2,1)}, u32[]{:S(2)}) copy-start(bf16[1,448,2048]{2,1,0:T(8,128)(2,1)} %param.12) | copy-start | bytes 5505028
  7.2 11.8 %copy-start.5 = (bf16[128,896]{1,0:T(8,128)(2,1)S(1)}, bf16[128,896]{1,0:T(8,128)(2,1)}, u32[]{:S(2)}) copy-start(bf16[128,896]{1,0:T(8,128)(2,1)} %param.7) | copy-start | bytes 688132
  12.6 20.8 %all-to-all-start.2 = ((bf16[8,64,896]{2,1,0:T(8,128)(2,1)}), bf16[8,64,896]{2,1,0:T(8,128)(2,1)S(1)}, u32[]{:S(2)}, u32[]{:S(2)}) async-start(bf16[8,64,896]{2,1,0:T(8,128)(2,1)} %bitcast.12), calls=%async_computation.2 | async-start | bytes 1835008 | tf_op jit(solution)/shard_map/all_to_all | solution.py:53
  33.4 0.9 copy-start.1
  34.3 63.0 %all-to-all-start = ((bf16[8,64,896]{2,1,0:T(8,128)(2,1)}), bf16[8,64,896]{2,1,0:T(8,128)(2,1)S(1)}, u32[]{:S(2)}, u32[]{:S(2)}) async-start(bf16[8,64,896]{2,1,0:T(8,128)(2,1)} %bitcast.5), calls=%async_computation | async-start | bytes 1835008 | tf_op jit(solution)/shard_map/all_to_all | solution.py:46
  97.3 66.6 %all-to-all-start.3 = ((bf16[16,2,14336]{2,1,0:T(2,128)(2,1)}), bf16[16,2,14336]{2,1,0:T(2,128)(2,1)}, u32[]{:S(2)}, u32[]{:S(2)}) async-start(bf16[16,2,14336]{2,1,0:T(2,128)(2,1)} %reshape.68), calls=%async_computation.3 | async-start | bytes 1835008 | tf_op jit(solution)/shard_map/all_to_all | solution.py:52
  163.9 29.7 %all-to-all-start.1 = ((bf16[16,2,14336]{2,1,0:T(2,128)(2,1)}), bf16[16,2,14336]{2,1,0:T(2,128)(2,1)}, u32[]{:S(2)}, u32[]{:S(2)}) async-start(bf16[16,2,14336]{2,1,0:T(2,128)(2,1)} %reshape.70), calls=%async_computation.1 | async-start | bytes 1835008 | tf_op jit(solution)/shard_map/all_to_all | solution.py:45
  171.2 185.0 %reduce-scatter.2.cloned.1.call-start = ((), (), s32[]{:S(2)}) async-start(), calls=%async_computation.7 | async-start | bytes 13369344 | tf_op jit(solution)/shard_map/reduce_scatter | solution.py:71
  214.6 2.4 copy-start.4
  214.6 2.4 copy-start.7
  217.0 2.4 copy-start.2
  217.0 2.4 copy-start.6
  233.0 0.7 copy-start.9
  233.0 216.9 %all-gather.2.cloned.1.call-start = ((), (), s32[]{:S(2)}) async-start(), calls=%async_computation.8 | async-start | bytes 13369344 | tf_op jit(solution)/shard_map/all_gather | solution.py:85
  449.9 4.4 copy-start.8
  473.0 19.9 %all-to-all-start.4 = ((bf16[16,2,14336]{2,1,0:T(2,128)(2,1)}), bf16[16,2,14336]{2,1,0:T(2,128)(2,1)S(1)}, u32[]{:S(2)}, u32[]{:S(2)}) async-start(bf16[16,2,14336]{2,1,0:T(2,128)(2,1)} %reshape.72), calls=%async_computation.5 | async-start | bytes 1835008 | tf_op jit(solution)/shard_map/all_to_all | solution.py:100
  556.6 18.8 %all-to-all-start.5 = ((bf16[8,2,28672]{2,1,0:T(2,128)(2,1)}), bf16[8,2,28672]{2,1,0:T(2,128)(2,1)S(1)}, u32[]{:S(2)}, u32[]{:S(2)}) async-start(bf16[8,2,28672]{2,1,0:T(2,128)(2,1)} %reshape.74), calls=%async_computation.6 | async-start | bytes 1835008 | tf_op jit(solution)/shard_map/all_to_all | solution.py:99
  561.0 5.9 copy-start.3
Sparse Core Ops, SparseCore 0:
  233.1 123.0 reduce-scatter.1
  359.5 90.3 all-gather.1
where the time goes:
time: 606 us; the launch traced here: 595 us
  waiting for transfers between devices  240 us (40%)
  other arithmetic  147 us (24%)
  local copies, waits for them, and re-layouts  122 us (20%)
  matrix products  37.9 us (6%)
  starting transfers between devices  34.6 us (6%)
  between operations  14.8 us (2%)
    unnamed x4, other arithmetic  131 us
    reduce_scatter x1, waiting for transfers between devices, body(): lax.psum_scatter(jnp.concatenate([gate, upper, back], axis=1).astype(jnp....  122 us
    all_gather x1, waiting for transfers between devices, body(): piece = lax.all_gather(local, 'dp', axis=0, tiled=True)  91.2 us
    unnamed x32, local copies, waits for them, and re-layouts  47.4 us
    all_to_all x2, local copies, waits for them, and re-layouts, body(): lax.all_to_all(send_g, 'expert', split_axis=0, concat_axis=2, tiled=True)  13.7 us
    all_to_all x1, waiting for transfers between devices, body(): lax.all_to_all(send_g, 'expert', split_axis=0, concat_axis=2, tiled=True)  13.1 us
    all_to_all x2, local copies, waits for them, and re-layouts, body(): lax.all_to_all(dx_rows.reshape(1, slots, shard_width), 'dp', split_axis=1...  12.8 us
    all_to_all x2, local copies, waits for them, and re-layouts, body(): lax.all_to_all(send_x, 'expert', split_axis=0, concat_axis=2, tiled=True)  12.8 us
  transfers between devices with their start and end apart: 8, of which 5 were waited for; matrix products, arithmetic and copies ran while one was open for 26% of the time, Pallas kernels for 0%

commit v1 on v0

--- a/solution.py
+++ b/solution.py
@@ -96,15 +96,12 @@
     ) + lax.dot_general(d_up, up_shard, last_dims, preferred_element_type=jnp.float32)
     dx_rows = block_dx.astype(jnp.bfloat16)
     grad_g, grad_u, grad_d, dx_rows = (grad_g, grad_u, grad_d, dx_rows)
-    returned = lax.all_to_all(
-        lax.all_to_all(
-            dx_rows.reshape(1, slots, shard_width), "dp", split_axis=1, concat_axis=2, tiled=True
-        ),
-        "expert",
-        split_axis=2,
-        concat_axis=0,
-        tiled=True,
+    x = lax.all_to_all(
+        dx_rows.reshape(1, slots, shard_width), "dp", split_axis=1, concat_axis=2, tiled=True
     )
+    pieces = jnp.split(x, lax.axis_size("expert"), axis=2)
+    got = lax.all_to_all(jnp.stack(pieces), "expert", 0, 0)
+    returned = jnp.concatenate(got, axis=0)
     returned = returned.reshape(experts * capacity, -1)
     grad_tokens = lax.dot_general(
         dispatch, returned, rows_first, preferred_element_type=jnp.float32

time: 606 us -> 551 us (0.909)
  other arithmetic: 147 us -> 106 us
  local copies, waits for them, and re-layouts: 122 us -> 108 us
    unnamed x4 -> x3, other arithmetic: 131 us -> 90.3 us
    all_to_all x2, local copies, waits for them, and re-layouts: 12.8 us -> 2.69 us  [body(): lax.all_to_all(dx_rows.reshape(1, slots, shard_width), 'dp', split_axis=1...]
    all_to_all x3 -> x0, local copies, waits for them, and re-layouts: 7.39 us -> none  [body(): lax.all_to_all(lax.all_to_all(dx_rows.reshape(1, slots, shard_width), 'dp...]
    unnamed x32 -> x36, local copies, waits for them, and re-layouts: 47.4 us -> 49.5 us
  transfers between devices with their start and end apart: 8 -> 8, of which waited for: 5 -> 5; matrix products, arithmetic and copies ran while one was open for 26% -> 29% of each run, Pallas kernels for 0% -> 0%
where the time goes in v1:
time: 551 us; the launch traced here: 540 us
  waiting for transfers between devices  240 us (44%)
  local copies, waits for them, and re-layouts  108 us (20%)
  other arithmetic  106 us (19%)
  matrix products  37.9 us (7%)
  starting transfers between devices  34.3 us (6%)
  between operations  14.5 us (3%)
    reduce_scatter x1, waiting for transfers between devices, body(): lax.psum_scatter(jnp.concatenate([gate, upper, back], axis=1).astype(jnp....  122 us
    all_gather x1, waiting for transfers between devices, body(): piece = lax.all_gather(local, 'dp', axis=0, tiled=True)  91.1 us
    unnamed x3, other arithmetic  90.3 us
    unnamed x36, local copies, waits for them, and re-layouts  49.5 us
    all_to_all x2, local copies, waits for them, and re-layouts, body(): lax.all_to_all(send_g, 'expert', split_axis=0, concat_axis=2, tiled=True)  13.7 us
    all_to_all x1, waiting for transfers between devices, body(): lax.all_to_all(send_g, 'expert', split_axis=0, concat_axis=2, tiled=True)  13.1 us
    all_to_all x2, local copies, waits for them, and re-layouts, body(): lax.all_to_all(send_x, 'expert', split_axis=0, concat_axis=2, tiled=True)  12.8 us
    all_to_all x3, local copies, waits for them, and re-layouts, body(): lax.all_to_all(lax.all_to_all(send_g, 'expert', split_axis=0, concat_axis...  12 us
  transfers between devices with their start and end apart: 8, of which 5 were waited for; matrix products, arithmetic and copies ran while one was open for 29% of the time, Pallas kernels for 0%

profile of v1, /device:TPU:1, one launch (start us, length us, event | category | flops | bytes accessed | tf_op | source)
XLA Modules:
  0.0 540.1 jit_solution(3937796443249993849)
XLA Ops:
  7.2 0.9 copy.71
  8.4 0.6 reduce-window.6
  9.6 0.7 compare_select_fusion
  10.3 2.2 convolution_convert_fusion.3
  12.6 6.4 %all-to-all-start.2 = ((bf16[8,64,896]{2,1,0:T(8,128)(2,1)}), bf16[8,64,896]{2,1,0:T(8,128)(2,1)S(1)}, u32[]{:S(2)}, u32[]{:S(2)}) async-start(bf16[8,64,896]{2,1,0:T(8,128)(2,1)} %bitcast.12), calls=%async_computation.2 | async-start | bytes 1835008 | tf_op jit(solution)/shard_map/all_to_all | solution.py:53
  19.0 1.3 convolution_convert_fusion.4
  20.3 13.1 %all-to-all-done.2 = bf16[8,64,896]{2,1,0:T(8,128)(2,1)S(1)} async-done(((bf16[8,64,896]{2,1,0:T(8,128)(2,1)}), bf16[8,64,896]{2,1,0:T(8,128)(2,1)S(1)}, u32[]{:S(2)}, u32[]{:S(2)}) %all-to-all-start.2) | async-done | bytes 917536 | tf_op jit(solution)/shard_map/all_to_all | solution.py:53
  33.4 0.9 copy-done.1
  34.3 3.6 all-to-all-start
  37.9 2.6 copy.86
  40.4 11.1 %reshape.60 = bf16[1,64,7168]{1,0,2:T(2,128)(2,1)} reshape(bf16[1,64,8,896]{1,3,2,0:T(8,128)(2,1)} %copy.86) | data formatting | bytes 1835008 | tf_op jit(solution)/shard_map/all_to_all | solution.py:53
  51.6 0.5 broadcast.46
  52.1 41.0 %reduce.2 = bf16[7168,64]{1,0:T(8,128)(2,1)} reduce(bf16[7168,1,64]{2,1,0:T(2,128)(2,1)} %bitcast.112, bf16[]{:T(256)} %broadcast.46), dimensions={1}, to_apply=%bitcast.93.reduce_sub_computation | reduce | bytes 1835010
  93.1 4.3 reshape.62
  97.4 8.5 %all-to-all-start.3 = ((bf16[16,2,14336]{2,1,0:T(2,128)(2,1)}), bf16[16,2,14336]{2,1,0:T(2,128)(2,1)}, u32[]{:S(2)}, u32[]{:S(2)}) async-start(bf16[16,2,14336]{2,1,0:T(2,128)(2,1)} %reshape.62), calls=%async_computation.3 | async-start | bytes 1835008 | tf_op jit(solution)/shard_map/all_to_all | solution.py:52
  105.9 1.7 copy.85
  107.5 11.1 %reshape.59 = bf16[1,64,7168]{1,0,2:T(2,128)(2,1)} reshape(bf16[1,64,8,896]{1,3,2,0:T(8,128)(2,1)} %copy.85) | data formatting | bytes 1835008 | tf_op jit(solution)/shard_map/all_to_all | solution.py:46
  118.6 41.0 %reduce.3 = bf16[7168,64]{1,0:T(8,128)(2,1)} reduce(bf16[7168,1,64]{2,1,0:T(2,128)(2,1)} %bitcast.113, bf16[]{:T(256)} %broadcast.46), dimensions={1}, to_apply=%bitcast.95.reduce_sub_computation | reduce | bytes 1835010
  159.6 4.3 reshape.64
  163.9 7.2 %all-to-all-start.1 = ((bf16[16,2,14336]{2,1,0:T(2,128)(2,1)}), bf16[16,2,14336]{2,1,0:T(2,128)(2,1)}, u32[]{:S(2)}, u32[]{:S(2)}) async-start(bf16[16,2,14336]{2,1,0:T(2,128)(2,1)} %reshape.64), calls=%async_computation.1 | async-start | bytes 1835008 | tf_op jit(solution)/shard_map/all_to_all | solution.py:45
  171.1 0.2 reduce-scatter.2.cloned.1.call-start
  171.4 9.9 %reshape.63 = bf16[7168,1,64]{2,1,0:T(2,128)(2,1)} reshape(bf16[16,2,14336]{2,1,0:T(2,128)(2,1)} %all-to-all-done.3) | data formatting | bytes 1835008
  181.3 8.1 %copy.80 = bf16[1,64,7168]{2,1,0:T(8,128)(2,1)} copy(bf16[1,64,7168]{1,0,2:T(2,128)(2,1)} %bitcast.114) | data formatting | bytes 1835008 | tf_op jit(solution)/shard_map/all_to_all | solution.py:52
  189.5 2.3 all_to_all.76
  191.8 1.5 copy.81
  193.4 9.9 %reshape.65 = bf16[7168,1,64]{2,1,0:T(2,128)(2,1)} reshape(bf16[16,2,14336]{2,1,0:T(2,128)(2,1)} %all-to-all-done.1) | data formatting | bytes 1835008
  203.3 8.1 %copy.76 = bf16[1,64,7168]{2,1,0:T(8,128)(2,1)} copy(bf16[1,64,7168]{1,0,2:T(2,128)(2,1)} %bitcast.115) | data formatting | bytes 1835008 | tf_op jit(solution)/shard_map/all_to_all | solution.py:45
  211.4 2.3 all_to_all.69
  213.8 0.6 copy.77
  214.4 2.3 convolution_convert_fusion.1
  216.8 2.3 convolution_convert_fusion.2
  219.1 2.3 convolution_convert_fusion
  221.5 11.5 %pad_maximum_fusion = bf16[1024,6144]{1,0:T(8,128)(2,1)} fusion(bf16[1024,2048]{1,0:T(8,128)(2,1)S(1)} %convolution_convert_fusion, bf16[1024,2048]{1,0:T(8,128)(2,1)S(1)} %convolution_convert_fusion.1, bf16[1024,2048]{1,0:T(8,128)(2,1)S(1)} %convolution_convert_fusion.2), kind=kLoop, calls=%fused_computation | loop fusion | flops 37748736 | bytes 25165824 | tf_op jit(solution)/shard_map/concatenate | solution.py:72
  233.0 0.4 all-gather.2.cloned.1.call-start
  233.9 122.2 %reduce-scatter.2.cloned.1.call-done = bf16[64,6144]{1,0:T(8,128)(2,1)} async-done(((bf16[1024,6144]{1,0:T(8,128)(2,1)}), bf16[64,6144]{1,0:T(8,128)(2,1)}) %reduce-scatter.2.cloned.1.call-update) | async-done | bytes 786448 | tf_op jit(solution)/shard_map/reduce_scatter | solution.py:71
  356.2 1.2 convert_element_type.43
  357.4 0.4 multiply_convert_fusion.5
  357.8 0.9 pad_maximum_fusion.1
  358.7 91.1 %all-gather.2.cloned.1.call-done = bf16[1024,6144]{1,0:T(8,128)(2,1)} async-done(((bf16[64,6144]{1,0:T(8,128)(2,1)}), bf16[1024,6144]{1,0:T(8,128)(2,1)}) %all-gather.2.cloned.1.call-update) | async-done | bytes 12582928 | tf_op jit(solution)/shard_map/all_gather | solution.py:85
  449.9 4.4 fusion.4
  454.3 4.4 fusion.34
  458.7 3.9 copy.82
  462.6 8.3 %reduce.4 = bf16[1024,448]{1,0:T(8,128)(2,1)S(1)} reduce(bf16[1024,1,448]{2,1,0:T(2,128)(2,1)} %bitcast.116, bf16[]{:T(256)} %broadcast.46), dimensions={1}, to_apply=%bitcast.97.reduce_sub_computation | reduce | bytes 1835010
  470.8 2.1 reshape.66
  472.9 3.8 all-to-all-start.4
  476.8 5.8 %fusion.16 = bf16[1,448,2048]{2,1,0:T(8,128)(2,1)} fusion(bf16[1024,448]{1,0:T(8,128)(2,1)} %bitcast.128, bf16[1024,6144]{1,0:T(8,128)(2,1)} %all-gather.2.cloned.1.call-done), kind=kOutput, calls=%fused_computation.17 | convolution fusion | flops 1880883200 | bytes 7077888 | tf_op jit(solution)/shard_map/dot_general | solution.py:91
  482.6 10.2 %all-to-all-done.4 = bf16[16,2,14336]{2,1,0:T(2,128)(2,1)S(1)} async-done(((bf16[16,2,14336]{2,1,0:T(2,128)(2,1)}), bf16[16,2,14336]{2,1,0:T(2,128)(2,1)S(1)}, u32[]{:S(2)}, u32[]{:S(2)}) %all-to-all-start.4) | async-done | bytes 917536 | tf_op jit(solution)/shard_map/all_to_all | solution.py:99
  492.8 3.7 reshape.67
  496.5 1.9 copy.89
  498.4 0.6 copy.83
  499.0 2.1 all_to_all.81
  501.1 1.6 fusion.48
  502.7 1.6 fusion.47
  504.2 1.5 fusion.46
  505.8 1.5 fusion.45
  507.3 1.6 fusion.44
  508.9 1.5 fusion.43
  510.4 1.6 fusion.42
  512.0 1.6 fusion.41
  513.5 4.1 all-to-all-start.5
  517.6 5.9 %fusion.19 = bf16[1,448,2048]{2,1,0:T(8,128)(2,1)} fusion(bf16[1024,448]{1,0:T(8,128)(2,1)} %bitcast.129, bf16[1024,6144]{1,0:T(8,128)(2,1)} %all-gather.2.cloned.1.call-done), kind=kOutput, calls=%fused_computation.18 | convolution fusion | flops 1880883200 | bytes 7077888 | tf_op jit(solution)/shard_map/dot_general | solution.py:92
  523.6 5.5 %fusion.22 = bf16[1,2048,448]{1,2,0:T(8,128)(2,1)} fusion(bf16[1024,448]{1,0:T(8,128)(2,1)S(1)} %bitcast.125, bf16[1024,6144]{1,0:T(8,128)(2,1)} %all-gather.2.cloned.1.call-done), kind=kOutput, calls=%fused_computation.19 | convolution fusion | flops 1880883200 | bytes 6946816 | tf_op jit(solution)/shard_map/dot_general | solution.py:93
  529.1 2.9 all-to-all-done.5
  532.0 1.0 convolution_convert_fusion.5
  (36 shorter events, 1.5 us)
Async XLA Ops:
  7.2 207.2 %copy-start = (bf16[1,448,2048]{2,1,0:T(8,128)(2,1)S(1)}, bf16[1,448,2048]{2,1,0:T(8,128)(2,1)}, u32[]{:S(2)}) copy-start(bf16[1,448,2048]{2,1,0:T(8,128)(2,1)} %param.12) | copy-start | bytes 5505028
  7.2 11.8 %copy-start.5 = (bf16[128,896]{1,0:T(8,128)(2,1)S(1)}, bf16[128,896]{1,0:T(8,128)(2,1)}, u32[]{:S(2)}) copy-start(bf16[128,896]{1,0:T(8,128)(2,1)} %param.7) | copy-start | bytes 688132
  12.6 20.8 %all-to-all-start.2 = ((bf16[8,64,896]{2,1,0:T(8,128)(2,1)}), bf16[8,64,896]{2,1,0:T(8,128)(2,1)S(1)}, u32[]{:S(2)}, u32[]{:S(2)}) async-start(bf16[8,64,896]{2,1,0:T(8,128)(2,1)} %bitcast.12), calls=%async_computation.2 | async-start | bytes 1835008 | tf_op jit(solution)/shard_map/all_to_all | solution.py:53
  33.4 0.9 copy-start.1
  34.3 63.1 %all-to-all-start = ((bf16[8,64,896]{2,1,0:T(8,128)(2,1)}), bf16[8,64,896]{2,1,0:T(8,128)(2,1)S(1)}, u32[]{:S(2)}, u32[]{:S(2)}) async-start(bf16[8,64,896]{2,1,0:T(8,128)(2,1)} %bitcast.5), calls=%async_computation | async-start | bytes 1835008 | tf_op jit(solution)/shard_map/all_to_all | solution.py:46
  97.4 66.6 %all-to-all-start.3 = ((bf16[16,2,14336]{2,1,0:T(2,128)(2,1)}), bf16[16,2,14336]{2,1,0:T(2,128)(2,1)}, u32[]{:S(2)}, u32[]{:S(2)}) async-start(bf16[16,2,14336]{2,1,0:T(2,128)(2,1)} %reshape.62), calls=%async_computation.3 | async-start | bytes 1835008 | tf_op jit(solution)/shard_map/all_to_all | solution.py:52
  163.9 29.4 %all-to-all-start.1 = ((bf16[16,2,14336]{2,1,0:T(2,128)(2,1)}), bf16[16,2,14336]{2,1,0:T(2,128)(2,1)}, u32[]{:S(2)}, u32[]{:S(2)}) async-start(bf16[16,2,14336]{2,1,0:T(2,128)(2,1)} %reshape.64), calls=%async_computation.1 | async-start | bytes 1835008 | tf_op jit(solution)/shard_map/all_to_all | solution.py:45
  171.1 185.0 %reduce-scatter.2.cloned.1.call-start = ((), (), s32[]{:S(2)}) async-start(), calls=%async_computation.7 | async-start | bytes 13369344 | tf_op jit(solution)/shard_map/reduce_scatter | solution.py:71
  214.4 2.4 copy-start.4
  214.4 2.4 copy-start.7
  216.8 2.4 copy-start.2
  216.8 2.4 copy-start.6
  233.0 0.7 copy-start.9
  233.0 216.9 %all-gather.2.cloned.1.call-start = ((), (), s32[]{:S(2)}) async-start(), calls=%async_computation.8 | async-start | bytes 13369344 | tf_op jit(solution)/shard_map/all_gather | solution.py:85
  449.9 4.4 copy-start.8
  472.9 19.9 %all-to-all-start.4 = ((bf16[16,2,14336]{2,1,0:T(2,128)(2,1)}), bf16[16,2,14336]{2,1,0:T(2,128)(2,1)S(1)}, u32[]{:S(2)}, u32[]{:S(2)}) async-start(bf16[16,2,14336]{2,1,0:T(2,128)(2,1)} %reshape.66), calls=%async_computation.5 | async-start | bytes 1835008 | tf_op jit(solution)/shard_map/all_to_all | solution.py:99
  513.5 18.5 %all-to-all-start.5 = ((bf16[8,1,64,896]{3,2,1,0:T(8,128)(2,1)}), bf16[8,1,64,896]{3,2,1,0:T(8,128)(2,1)S(1)}, u32[]{:S(2)}, u32[]{:S(2)}) async-start(bf16[8,1,64,896]{3,2,1,0:T(8,128)(2,1)} %fusion.41), calls=%async_computation.6 | async-start | bytes 1835008 | tf_op jit(solution)/shard_map/all_to_all | solution.py:103
  517.6 5.9 %copy-start.3 = (bf16[1,16,64,448]{3,2,1,0:T(8,128)(2,1)S(1)}, bf16[1,16,64,448]{3,2,1,0:T(8,128)(2,1)}, u32[]{:S(2)}) copy-start(bf16[1,16,64,448]{3,2,1,0:T(8,128)(2,1)} %copy.81) | copy-start | bytes 2752516
Sparse Core Ops, SparseCore 0:
  233.1 123.0 reduce-scatter.1
  359.5 90.3 all-gather.1
